TPU v7x, 512 devices: a whole 4x8x8 slice. The times are simulated.
512 devices in a mesh: row: 32 (over x, y), col: 16 (over z, core).
Axes of the slice: x: 4, y: 8, z: 8, core: 2. Of those that a mesh axis runs over, the one named last changes fastest.
Arguments:
- hessian: float32 [2, 8192, 4, 4096], P(None, 'row', None, 'col'), as said below
Outputs:
- factored: float32 [2, 8192, 4, 4096], P(None, 'row', None, 'col')
Inputs may be any that keep to these rules, and one draw needn't show every extreme that they name: hessian, read as the 16384 x 16384 matrix H0, is symmetric and positive definite.
All inputs are finite; a program needn't handle non-finite values.
Results may differ from a plain program's by a relative error of at most 0.0003.
Values sent between devices are 32-bit elements; how exact they have to be, the bound alone decides.
A program may use at most 64 MiB of HBM per device.

v0:
```python
import jax
import jax.numpy as jnp
from jax import lax
from jax.sharding import PartitionSpec as P


def broadcast(x, axis, root):
    mine = lax.axis_index(axis) == root
    return lax.psum(jnp.where(mine, x, jnp.zeros_like(x)), axis)


def invert_factor(diagonal):
    lower_factor = jnp.linalg.cholesky(diagonal)
    identity = jnp.eye(diagonal.shape[0], dtype=diagonal.dtype)
    return lax.linalg.triangular_solve(lower_factor, identity, left_side=True, lower=True)


def outer_update(own_panel, across):
    row_cycles, block_width, depth = own_panel.shape
    column_count = across.shape[0]
    product_flat = jnp.dot(
        own_panel.reshape(row_cycles * block_width, depth),
        across.reshape(column_count * block_width, depth).T,
        precision=lax.Precision.HIGHEST,
    )
    return product_flat.reshape(row_cycles, block_width, column_count, block_width)


def on_device(hessian):
    row_count = lax.axis_size("row")
    column_count = lax.axis_size("col")
    row_index = lax.axis_index("row")
    column_index = lax.axis_index("col")
    row_cycles, block_width, column_cycles, _ = hessian.shape
    row_blocks = row_index + row_count * jnp.arange(row_cycles, dtype=jnp.int32)
    col_blocks = column_index + column_count * jnp.arange(column_cycles, dtype=jnp.int32)
    offsets = jnp.arange(block_width, dtype=jnp.int32)
    row_position = row_blocks[:, None] * block_width + offsets[None, :]

    def apply_factor(column, inverse, panel_index):
        own_panel = jnp.dot(
            column.reshape(row_cycles * block_width, block_width),
            inverse.T,
            precision=lax.Precision.HIGHEST,
        )
        own_panel = own_panel.reshape(row_cycles, block_width, block_width)
        keep_mask = row_position[:, :, None] >= panel_index * block_width + offsets[None, None, :]
        return jnp.where(keep_mask, own_panel, jnp.zeros_like(own_panel))

    def spread_rows(own_panel):
        depth = own_panel.shape[2]
        pieces = []
        for root_half in range(2):
            pieces.append(broadcast(own_panel, "row", column_index + root_half * column_count))
        across = jnp.stack(pieces, axis=1)
        return across.reshape(column_cycles, block_width, depth)

    def make_panel(matrix, panel_index):
        column_slab = matrix[:, :, panel_index // column_count, :]
        column = broadcast(column_slab, "col", panel_index % column_count)
        diagonal = broadcast(column[panel_index // row_count], "row", panel_index % row_count)
        inverse = invert_factor(diagonal)
        own_panel = apply_factor(column, inverse, panel_index)
        return (own_panel, spread_rows(own_panel))

    matrix = hessian
    first_panel, first_across = make_panel(matrix, 0)
    matrix = matrix - outer_update(first_panel, first_across)
    second_panel, second_across = make_panel(matrix, 1)
    matrix = matrix - outer_update(second_panel, second_across)
    row_global = row_blocks[:, None, None, None]
    col_global = col_blocks[None, None, :, None]
    result = jnp.where(row_global < 2, jnp.zeros_like(matrix), matrix)
    result = jnp.where(col_global == 0, first_panel[:, :, None, :], result)
    result = jnp.where(col_global == 1, second_panel[:, :, None, :], result)
    return result


def solution(mesh):
    in_specs = (P(None, "row", None, "col"),)
    out_specs = P(None, "row", None, "col")
    return jax.shard_map(
        on_device, mesh=mesh, in_specs=in_specs, out_specs=out_specs, check_vma=False
    )
```

profile of v0, /device:TPU:64, one launch (start us, length us, event | category | flops | bytes accessed | tf_op | source)
XLA Modules:
  0.0 1026.2 jit_solution(2998131894410887725)
XLA Ops:
  6.5 1.9 copy.17
  9.4 117.4 %all-reduce.10.cloned.1.call-done = f32[2,256,256]{1,2,0:T(8,128)} async-done(((f32[2,256,256]{1,2,0:T(8,128)}), f32[2,256,256]{1,2,0:T(8,128)}) %all-reduce.10.cloned.1.call-update) | async-done | bytes 524304 | tf_op jit(solution)/shard_map/psum | solution.py:9
  126.8 1.7 fusion.5
  128.7 159.6 %all-reduce.12.cloned.1.call-done = f32[256,256]{0,1:T(8,128)} async-done(((f32[256,256]{0,1:T(8,128)}), f32[256,256]{0,1:T(8,128)}) %all-reduce.12.cloned.1.call-update) | async-done | bytes 262160 | tf_op jit(solution)/shard_map/psum | solution.py:9
  290.4 11.7 %cholesky.130 = f32[128,128]{1,0:T(8,128)S(1)} custom-call(f32[128,128]{1,0:T(8,128)S(1)} %cholesky.194), custom_call_target="Cholesky" | custom-call | tf_op jit(solution)/shard_map/jit(cholesky)/cholesky | solution.py:13
  302.1 9.8 custom-call.13
  314.1 11.7 %cholesky.147 = f32[128,128]{1,0:T(8,128)S(1)} custom-call(f32[128,128]{1,0:T(8,128)S(1)} %convolution_subtract_fusion.4), custom_call_target="Cholesky" | custom-call | tf_op jit(solution)/shard_map/jit(cholesky)/cholesky | solution.py:13
  327.8 4.0 while.4
  331.9 19.7 %custom-call.14 = f32[2,128,128]{1,2,0:T(8,128)S(1)} custom-call(f32[2,128,128]{2,1,0:T(8,128)S(1)} %get-tuple-element.21), custom_call_target="InvertDiagBlocksLowerTriangular" | custom-call | tf_op jit(solution)/shard_map/triangular_solve/custom-call.0 | solution.py:15
  354.6 158.0 %all-reduce.20.cloned.1.call-done = (f32[2,1,256,256]{3,2,0,1:T(8,128)}, f32[2,1,256,256]{3,2,0,1:T(8,128)}) async-done(((f32[2,1,256,256]{3,2,0,1:T(8,128)}, f32[2,1,256,256]{3,2,0,1:T(8,128)}), (f32[2,1,256,256]{3,2,0,1:T(8,128)}, f32[2,1,256,256]{3,2,0,1:T(8,128)})) %all-reduce.20.cloned.1.call-update) | async-done | bytes 1048592 | tf_op jit(solution)/shard_map/psum | solution.py:9
  514.0 2.0 convolution_subtract_fusion
  515.9 1.3 copy-done
  518.2 110.9 %all-reduce.14.cloned.1.call-done = f32[2,256,256]{1,2,0:T(8,128)} async-done(((f32[2,256,256]{1,2,0:T(8,128)}), f32[2,256,256]{1,2,0:T(8,128)}) %all-reduce.14.cloned.1.call-update) | async-done | bytes 524304 | tf_op jit(solution)/shard_map/psum | solution.py:9
  629.0 1.7 fusion.4
  630.8 159.1 %all-reduce.16.cloned.1.call-done = f32[256,256]{0,1:T(8,128)} async-done(((f32[256,256]{0,1:T(8,128)}), f32[256,256]{0,1:T(8,128)}) %all-reduce.16.cloned.1.call-update) | async-done | bytes 262160 | tf_op jit(solution)/shard_map/psum | solution.py:9
  792.0 11.7 %cholesky.164 = f32[128,128]{1,0:T(8,128)S(1)} custom-call(f32[128,128]{1,0:T(8,128)S(1)} %cholesky.197), custom_call_target="Cholesky" | custom-call | tf_op jit(solution)/shard_map/jit(cholesky)/cholesky | solution.py:13
  803.8 9.8 custom-call.15
  814.1 11.7 %cholesky.181 = f32[128,128]{1,0:T(8,128)S(1)} custom-call(f32[128,128]{1,0:T(8,128)S(1)} %convolution_subtract_fusion.3), custom_call_target="Cholesky" | custom-call | tf_op jit(solution)/shard_map/jit(cholesky)/cholesky | solution.py:13
  828.4 4.0 while.5
  832.5 19.7 %custom-call.16 = f32[2,128,128]{1,2,0:T(8,128)S(1)} custom-call(f32[2,128,128]{2,1,0:T(8,128)S(1)} %get-tuple-element.22), custom_call_target="InvertDiagBlocksLowerTriangular" | custom-call | tf_op jit(solution)/shard_map/triangular_solve/custom-call.0 | solution.py:15
  856.4 156.8 %all-reduce.18.cloned.1.call-done = (f32[2,1,256,256]{3,2,0,1:T(8,128)}, f32[2,1,256,256]{3,2,0,1:T(8,128)}) async-done(((f32[2,1,256,256]{3,2,0,1:T(8,128)}, f32[2,1,256,256]{3,2,0,1:T(8,128)}), (f32[2,1,256,256]{3,2,0,1:T(8,128)}, f32[2,1,256,256]{3,2,0,1:T(8,128)})) %all-reduce.18.cloned.1.call-update) | async-done | bytes 1048592 | tf_op jit(solution)/shard_map/psum | solution.py:9
  1013.3 1.4 pad_maximum_fusion.1
  1015.3 2.3 select_select_fusion
  1017.6 1.8 copy.25
  (83 shorter events, 27.8 us)
Async XLA Ops:
  6.5 120.3 %all-reduce.10.cloned.1.call-start = ((), (), s32[]{:S(2)}) async-start(), calls=%async_computation | async-start | bytes 1048576 | tf_op jit(solution)/shard_map/psum | solution.py:9
  9.3 278.9 %all-reduce.12.cloned.1.call-start = ((), (), s32[]{:S(2)}) async-start(), calls=%async_computation.1 | async-start | bytes 524288 | tf_op jit(solution)/shard_map/psum | solution.py:9
  128.5 384.1 %all-reduce.20.cloned.1.call-start = ((), (), s32[]{:S(2)}) async-start(), calls=%async_computation.5 | async-start | bytes 2097152 | tf_op jit(solution)/shard_map/psum | solution.py:9
  290.3 11.8 %copy-start.5 = (f32[256,256]{1,0:T(8,128)}, f32[256,256]{1,0:T(8,128)S(1)}, u32[]{:S(2)}) copy-start(f32[256,256]{1,0:T(8,128)S(1)} %fusion.11) | copy-start | bytes 786436
  290.3 62.1 %copy-start.3 = (f32[2,256,256]{1,2,0:T(8,128)S(1)}, f32[2,256,256]{1,2,0:T(8,128)}, u32[]{:S(2)}) copy-start(f32[2,256,256]{1,2,0:T(8,128)} %all-reduce.10.cloned.1.call-done) | copy-start | bytes 1572868
  354.6 274.5 %all-reduce.14.cloned.1.call-start = ((), (), s32[]{:S(2)}) async-start(), calls=%async_computation.2 | async-start | bytes 1048576 | tf_op jit(solution)/shard_map/psum | solution.py:9
  515.9 1.3 copy-start
  518.1 271.8 %all-reduce.16.cloned.1.call-start = ((), (), s32[]{:S(2)}) async-start(), calls=%async_computation.3 | async-start | bytes 524288 | tf_op jit(solution)/shard_map/psum | solution.py:9
  630.7 382.5 %all-reduce.18.cloned.1.call-start = ((), (), s32[]{:S(2)}) async-start(), calls=%async_computation.4 | async-start | bytes 2097152 | tf_op jit(solution)/shard_map/psum | solution.py:9
  792.0 61.1 %copy-start.4 = (f32[2,256,256]{1,2,0:T(8,128)S(1)}, f32[2,256,256]{1,2,0:T(8,128)}, u32[]{:S(2)}) copy-start(f32[2,256,256]{1,2,0:T(8,128)} %all-reduce.14.cloned.1.call-done) | copy-start | bytes 1572868
  1013.3 1.9 copy-start.1
  1013.3 2.0 copy-start.2
Sparse Core Ops, SparseCore 0:
  9.7 117.1 all-reduce.9
  130.7 157.5 all-reduce.11
  354.7 157.8 all-reduce.19
  518.2 110.7 all-reduce.13
  632.3 157.5 all-reduce.15
  855.3 157.8 all-reduce.17
where the time goes:
time: 1030 us
  waiting for transfers between devices  862 us (84%)
  other arithmetic  120 us (12%)
  local copies, waits for them, and re-layouts  16.7 us (2%)
  between operations  16.3 us (2%)
  matrix products  10.7 us (1%)
    psum x6, waiting for transfers between devices, broadcast(): return lax.psum(jnp.where(mine, x, jnp.zeros_like(x)), axis)  862 us
    another operation x13, other arithmetic, invert_factor(): lower_factor = jnp.linalg.cholesky(diagonal)  68.6 us
    another operation x5, other arithmetic, invert_factor(): lax.linalg.triangular_solve(lower_factor, identity, left_side=True, lower...  39.4 us
  transfers between devices with their start and end apart: 6, of which 6 were waited for; matrix products, arithmetic and copies ran while one was open for 0% of the time, Pallas kernels for 0%

commit v1 on v0

v1 whole, which is shorter than its diff:
```python
import functools

import jax
import jax.numpy as jnp
from jax import lax
from jax.experimental import pallas as pl
from jax.experimental.pallas import tpu as pltpu
from jax.sharding import PartitionSpec as P

F = jnp.float32
HI = lax.Precision.HIGHEST
MESH = pl.DeviceIdType.MESH
W = 256


def recip(p):
    r = pl.reciprocal(p, approx=True)
    return r * (2.0 - p * r)

def leaf(m):
    m = list(m)
    sub = lax.broadcasted_iota(jnp.int32, (8, 128), 0)
    out = []
    for g in range(8):
        c = [[jnp.broadcast_to(m[v][:, 64 + 8 * g + k:65 + 8 * g + k], (8, 128)) for v in range(g, 8)] for k in range(8)]
        top = m[g]
        pivots = jnp.ones((8, 128), F)
        scaled_rows = []
        for k in range(8):
            col = c[k]
            pivot = jnp.broadcast_to(col[0][k:k + 1, :], (8, 128))
            r = recip(pivot)
            row = jnp.broadcast_to(top[k:k + 1, :], (8, 128)) * r
            scaled_rows.append(row)
            pivots = jnp.where(sub == k, pivot, pivots)
            top = top - jnp.where(sub > k, col[0], 0.0) * row
            for n in range(k + 1, 8):
                s = jnp.broadcast_to(col[0][n:n + 1, :], (8, 128)) * r
                c[n] = [a - b * s for a, b in zip(c[n], col)]
        for v in range(g + 1, 8):
            acc = m[v]
            for k in range(8):
                acc = acc - c[k][v - g] * scaled_rows[k]
            m[v] = acc
        out.append(top * lax.rsqrt(pivots))
    return out

class Comm:
    def __init__(self, nx, ny, nz, h, hv, rsrc, cbuf, rbuf, vbuf, dbuf, sems):
        self.nx, self.ny, self.nz = nx, ny, nz
        self.h, self.hv, self.rsrc, self.cbuf, self.rbuf = h, hv, rsrc, cbuf, rbuf
        self.vbuf, self.dbuf = vbuf, dbuf
        self.sems = sems
        self.row = lax.axis_index("row")
        self.col = lax.axis_index("col")
        self.x, self.y = self.row // ny, self.row % ny
        self.z, self.k = self.col // 2, self.col % 2
        self.root = jnp.logical_and(self.row == 0, self.col == 0)

    def at(self, x=None, y=None, z=None, k=None):
        x = self.x if x is None else x
        y = self.y if y is None else y
        z = self.z if z is None else z
        k = self.k if k is None else k
        return (x * self.ny + y, z * 2 + k)

    def barrier(self):
        nx, ny, nz = self.nx, self.ny, self.nz
        sem = pltpu.get_barrier_semaphore()

        def tell(device):
            pl.semaphore_signal(sem, inc=1, device_id=device, device_id_type=MESH)

        for root in range(2):
            pl.when(self.row != root)(lambda root=root: tell((root, self.col)))
        pl.when(self.z != 0)(lambda: tell(self.at(z=0)))
        tell(self.at(k=1 - self.k))
        for d in (1, -1):
            tell(self.at(y=(self.y + d) % ny))
            tell(self.at(z=(self.z + d) % nz))
        for d in range(1, nx):
            tell(self.at(x=(self.x + d) % nx))
        pl.when(self.root)(lambda: tell((1, 1)))
        total = 5 + nx - 1
        total = total + jnp.where(self.row < 2, nx * ny - 1, 0) + jnp.where(self.z == 0, nz - 1, 0)
        total = total + jnp.where(self.d_source(1), 1, 0)
        pl.semaphore_wait(sem, total)

    def remote(self, src, dst, send, recv, device):
        return pltpu.make_async_remote_copy(
            src_ref=src, dst_ref=dst, send_sem=send, recv_sem=recv, device_id=device, device_id_type=MESH
        )

    def scatter_c(self):
        nx, ny = self.nx, self.ny
        n = nx * ny
        sems_s, sems_r, local = self.sems["cs_send"], self.sems["cs_recv"], self.sems["local"]
        size = self.cbuf.shape[3]
        for root in range(2):

            @pl.when(self.row == root)
            def _(root=root):
                def send(i, carry):
                    p = (i % nx) * ny + (i // nx + root) % ny
                    copy = self.remote(
                        self.h.at[pl.ds(p * size, size)],
                        self.cbuf.at[root, p // ny, p % ny],
                        sems_s.at[p], sems_r.at[root], (p, self.col),
                    )
                    pl.when(p != root)(copy.start)
                    return carry
                lax.fori_loop(0, n, send, 0)
                pltpu.make_async_copy(
                    self.h.at[pl.ds(root * size, size)], self.cbuf.at[root, 0, root], local.at[root]
                ).start()

    def scatter_c_wait(self, root):
        size = self.cbuf.shape[3]

        @pl.when(self.row == root)
        def _():
            pltpu.make_async_copy(
                self.h.at[pl.ds(root * size, size)], self.cbuf.at[root, 0, root], self.sems["local"].at[root]
            ).wait()

        @pl.when(self.row != root)
        def _():
            piece = self.cbuf.at[root, self.x, self.y]
            self.remote(piece, piece, self.sems["cs_send"].at[0], self.sems["cs_recv"].at[root], self.at()).wait_recv()

    def scatter_c_done(self):
        size = self.cbuf.shape[3]
        for root in range(2):

            @pl.when(self.row == root)
            def _(root=root):
                def done(p, carry):
                    copy = self.remote(
                        self.h.at[pl.ds(p * size, size)], self.cbuf.at[root, p // self.ny, p % self.ny],
                        self.sems["cs_send"].at[p], self.sems["cs_recv"].at[root], (p, self.col),
                    )
                    pl.when(p != root)(copy.wait_send)
                    return carry
                lax.fori_loop(0, self.nx * self.ny, done, 0)

    def scatter_r_copy(self, q):
        return self.remote(
            self.rsrc.at[q], self.rbuf.at[self.k, q], self.sems["rs_send"].at[q], self.sems["rs_recv"], self.at(z=q)
        )

    def scatter_r_local(self):
        return [
            pltpu.make_async_copy(self.rsrc.at[0], self.rbuf.at[kk, 0], self.sems["local"].at[2]) for kk in range(2)
        ]

    def scatter_r(self):
        @pl.when(self.z == 0)
        def _():
            for q in range(1, self.nz):
                self.scatter_r_copy(q).start()
            for kk in range(2):
                pl.when(self.k == kk)(self.scatter_r_local()[kk].start)

    def scatter_r_wait(self):
        @pl.when(self.z == 0)
        def _():
            for kk in range(2):
                pl.when(self.k == kk)(self.scatter_r_local()[kk].wait)

        @pl.when(self.z != 0)
        def _():
            piece = self.rbuf.at[self.k, self.z]
            self.remote(piece, piece, self.sems["rs_send"].at[0], self.sems["rs_recv"], self.at()).wait_recv()

    def scatter_r_done(self):
        @pl.when(self.z == 0)
        def _():
            for q in range(1, self.nz):
                self.scatter_r_copy(q).wait_send()

    def ring(self, name, n, me, device, piece, step):
        half = n // 2
        out = []
        for way, sign in enumerate((1, -1)):
            index = (me - sign * (step - 1)) % n
            ref = piece(index, way if step == half else None)
            send = self.sems[name].at[0, way, step - 1]
            recv = self.sems[name].at[1, way, step - 1]
            out.append(self.remote(ref, ref, send, recv, device((me + sign) % n)))
        return out

    def ring_start(self, name, *args):
        for copy in self.ring(name, *args):
            copy.start()

    def ring_wait(self, name, n, me, device, piece, step):
        half = n // 2
        for way, sign in enumerate((1, -1)):
            index = (me - sign * step) % n
            ref = piece(index, way if step == half else None)
            send = self.sems[name].at[0, way, step - 1]
            recv = self.sems[name].at[1, way, step - 1]
            self.remote(ref, ref, send, recv, device((me + sign) % n)).wait_recv()

    def ring_done(self, name, *args):
        for copy in self.ring(name, *args):
            copy.wait_send()

    def rings(self):
        c = self.cbuf
        hs = c.shape[3] // 2
        hr = self.rbuf.shape[3] // 2

        def px0(i, h):
            ref = c.at[0, i, self.y]
            return ref if h is None else ref.at[pl.ds(h * hs, hs)]

        def py0(i, h):
            if h is None:
                return c.at[0, :, i]
            return c.at[0, :, i, pl.ds(h * hs, hs)]

        def py1(i, h):
            ref = c.at[1, self.x, i]
            return ref if h is None else ref.at[pl.ds(h * hs, hs)]

        def px1(i, h):
            if h is None:
                return c.at[1, i]
            return c.at[1, i, pl.ds(h * (self.ny // 2), self.ny // 2)]

        def pz(i, h):
            if h is None:
                return self.rbuf.at[self.k, i]
            return self.rbuf.at[self.k, i, h]

        dx = lambda i: self.at(x=i)
        dy = lambda i: self.at(y=i)
        dz = lambda i: self.at(z=i)
        return {
            "x0": ("x0", self.nx, self.x, dx, px0),
            "y0": ("y0", self.ny, self.y, dy, py0),
            "y1": ("y1", self.ny, self.y, dy, py1),
            "x1": ("x1", self.nx, self.x, dx, px1),
            "z": ("z", self.nz, self.z, dz, pz),
        }

    def swap_copy(self, kk):
        return self.remote(
            self.rbuf.at[kk], self.rbuf.at[kk], self.sems["swap"].at[0], self.sems["swap"].at[1], self.at(k=1 - self.k)
        )

    def swap_start(self):
        for kk in range(2):
            pl.when(self.k == kk)(self.swap_copy(kk).start)

    def swap_wait(self):
        for kk in range(2):
            pl.when(self.k != kk)(self.swap_copy(kk).wait_recv)

    def swap_done(self):
        for kk in range(2):
            pl.when(self.k == kk)(self.swap_copy(kk).wait_send)

    def prepare(self):
        @pl.when(self.z == 0)
        def _():
            nq, _, size, _ = self.rsrc.shape
            for q in range(nq):
                for ct in range(2):
                    self.rsrc[q, ct] = self.hv[pl.ds(q * size * 8 + ct * 4, size, stride=8), :]

    def d_source(self, b):
        return jnp.logical_and(self.row == b, self.col == 1)

    def d_copy(self, b):
        return self.remote(
            self.rsrc.at[pl.ds(0, self.dbuf.shape[1])], self.dbuf.at[b], self.sems["d"].at[0], self.sems["d"].at[1 + b], (0, 0)
        )

    def d_send(self):
        for b in range(2):
            pl.when(self.d_source(b))(lambda b=b: self.d_copy(b).start())

    def d_done(self):
        for b in range(2):
            pl.when(self.d_source(b))(lambda b=b: self.d_copy(b).wait_send())

    def v_stages(self, j):
        chunk = self.vbuf.at[j, 0] if j < 4 else self.vbuf.at[j]
        send, recv = self.sems["v_send"], self.sems["v_recv"].at[j]
        first = self.k == 0
        on_x = jnp.logical_and(first, self.x == 0)
        on_z = jnp.logical_and(on_x, self.z == 0)
        plan, base = [], 0
        for on, n, place in (
            (self.root, self.ny, lambda d: self.at(y=d)),
            (on_z, self.nz, lambda d: self.at(z=d)),
            (on_x, self.nx, lambda d: self.at(x=d)),
            (first, 2, lambda d: self.at(k=d)),
        ):
            plan.append((on, [functools.partial(self.remote, chunk, chunk, send.at[j, base + d - 1], recv, place(d)) for d in range(1, n)]))
            base += n - 1
        return plan

    def v_wait(self, j):
        plan = self.v_stages(j)
        pl.when(jnp.logical_not(self.root))(lambda: plan[3][1][0]().wait_recv())

    def v_send(self, j, wait):
        if wait:
            self.v_wait(j)
        for on, copies in self.v_stages(j):
            @pl.when(on)
            def _(copies=copies):
                for copy in copies:
                    copy().start()

    def v_done(self, j):
        for on, copies in self.v_stages(j):
            @pl.when(on)
            def _(copies=copies):
                for copy in copies:
                    copy().wait_send()

    def sequences(self):
        steps = {"x": self.nx // 2, "y": self.ny // 2, "z": self.nz // 2}
        names = (("x0", "y0"), ("y1", "x1"), ("z",))
        return [[(n, t) for n in chain for t in range(1, steps[n[0]] + 1)] for chain in names]

    def slot(self, s):
        r = self.rings()
        for i, chain in enumerate(self.sequences()):
            if s == 0:
                (self.scatter_r_wait if i == 2 else functools.partial(self.scatter_c_wait, i))()
            elif s <= len(chain):
                self.ring_wait(*r[chain[s - 1][0]], chain[s - 1][1])
            if s < len(chain):
                self.ring_start(*r[chain[s][0]], chain[s][1])
            if i == 2 and s == len(chain):
                self.swap_start()
        if s == self.slots() - 1:
            self.swap_wait()

    def slots(self):
        return 1 + max(len(chain) for chain in self.sequences())

    def finish(self):
        r = self.rings()
        for chain in self.sequences():
            for name, step in chain:
                self.ring_done(*r[name], step)
        self.scatter_c_done()
        self.scatter_r_done()
        self.swap_done()
        self.d_done()
        for j in range(8):
            self.v_done(j)


NAMES = ("local", "cs_send", "cs_recv", "rs_send", "rs_recv", "x0", "y0", "y1", "x1", "z", "swap", "d", "v_send", "v_recv")


def semaphores(nx, ny, nz):
    dma = pltpu.SemaphoreType.DMA
    shapes = {
        "local": (6,), "cs_send": (nx * ny,), "cs_recv": (2,), "rs_send": (nz,), "rs_recv": (),
        "x0": (2, 2, nx // 2), "y0": (2, 2, ny // 2), "y1": (2, 2, ny // 2), "x1": (2, 2, nx // 2),
        "z": (2, 2, nz // 2), "swap": (2,), "d": (3,), "v_send": (8, nx + ny + nz - 2), "v_recv": (8,),
    }
    return [dma(shapes[name]) for name in NAMES]


def dot(a, b):
    return jnp.dot(a, b, precision=HI, preferred_element_type=F)


def dot_t(a, b):
    return lax.dot_general(a, b, (((1,), (1,)), ((), ())), precision=HI, preferred_element_type=F)


def t_dot(a, b):
    return lax.dot_general(a, b, (((0,), (0,)), ((), ())), precision=HI, preferred_element_type=F)


def eye(n):
    return (lax.broadcasted_iota(jnp.int32, (n, n), 0) == lax.broadcasted_iota(jnp.int32, (n, n), 1)).astype(F)


def tiles(ref):
    q, _, rows, _ = ref.shape
    return jnp.concatenate([ref[:, ct].reshape(q * rows, 128) for ct in range(2)], axis=1)


def factor(c, s, hook):
    vbuf = c.vbuf
    s[:, 0:W] = eye(W)
    s[:, W:2 * W] = jnp.zeros((W, W), F)
    s[:, 2 * W:3 * W] = tiles(c.rsrc.at[pl.ds(0, 4)])
    for p in range(2):
        if p == 1:
            v00 = s[:, 0:W]
            for b in range(2):
                c.d_copy(b).wait_recv()
            u01 = dot(v00, tiles(c.dbuf.at[0]))
            s[:, 0:W] = -t_dot(u01, v00)
            s[:, W:2 * W] = eye(W)
            s[:, 2 * W:3 * W] = tiles(c.dbuf.at[1]) - t_dot(u01, u01)
        for i in range(4):
            lo, hi = 64 * i, 64 * i + 64
            m = jnp.concatenate([eye(64), s[lo:hi, 2 * W + lo:2 * W + hi]], axis=1)
            rows = leaf([m[8 * v:8 * v + 8, :] for v in range(8)])
            w = jnp.concatenate(rows, axis=0)[:, 0:64]
            r = dot(w, s[lo:hi, :])
            j = 4 * p + i
            vbuf[j, 0] = r[:, 0:W]
            if p == 1:
                vbuf[j, 1] = r[:, W:2 * W]
            c.v_send(j, False)
            if i < 3:
                col = dot_t(s[hi:W, 2 * W + lo:2 * W + hi], w)
                s[hi:W, :] = s[hi:W, :] - dot(col, r)
            s[lo:hi, :] = r
            hook(j)


def split(a):
    high = a.astype(jnp.bfloat16)
    return high, (a - high.astype(F)).astype(jnp.bfloat16)


def v_rows(c, p):
    return [jnp.concatenate([c.vbuf[4 * p + i, k] for i in range(4)], axis=0) for k in range(p + 1)]


def panel_rows(c, p, pr, rcat):
    parts = [dot_t(tiles(c.rbuf.at[k]), v) for k, v in enumerate(v_rows(c, p))]
    own = parts[0] if p == 0 else parts[0] + parts[1]
    pr[p] = own

    @pl.when(c.row < 2)
    def _():
        place = lax.broadcasted_iota(jnp.int32, (W, W), 0) + c.row * W
        keep = place >= lax.broadcasted_iota(jnp.int32, (W, W), 1) + p * W
        pr[p, 0:W] = jnp.where(keep, pr[p, 0:W], 0.0)

    high, low = split(pr[p])
    rcat[:, p * W:(p + 1) * W] = high
    rcat[:, (2 + p) * W:(3 + p) * W] = high
    rcat[:, (4 + p) * W:(5 + p) * W] = low


def panel_columns(c, p, ccat):
    vs = v_rows(c, p)
    for ct in range(2):
        for pair in range(2):
            lanes = [ct * 4 + 2 * pair, ct * 4 + 2 * pair + 1]
            total = None
            for k, v in enumerate(vs):
                a = jnp.concatenate(
                    [c.cbuf[k, :, :, pl.ds(t, 8, stride=8), :].reshape(W, 128) for t in lanes], axis=1
                )
                part = dot(v, a)
                total = part if total is None else total + part
            if pair == 0:
                place = lax.broadcasted_iota(jnp.int32, (W, 2 * 128), 1)
                place = jnp.where(place < 128, place + ct * 128 + c.col * W, 2 * W)
                keep = place >= lax.broadcasted_iota(jnp.int32, (W, 2 * 128), 0) + p * W
                total = jnp.where(keep, total, 0.0)
            high, low = split(total)
            at = slice(lanes[0] * 128, lanes[0] * 128 + 256)
            ccat[p * W:(p + 1) * W, at] = high
            ccat[(2 + p) * W:(3 + p) * W, at] = low
            ccat[(4 + p) * W:(5 + p) * W, at] = high


def update(c, out, pr, rcat, ccat):
    step = 128
    for part in range(4):
        rows = slice(part * step, part * step + step)
        for pair in range(4):
            product = jnp.dot(rcat[rows, :], ccat[:, pair * 256:pair * 256 + 256], preferred_element_type=F)
            for half in range(2):
                at = (pl.ds(part * step * 8 + pair * 2 + half, step, stride=8), slice(None))
                c.hv[at] = c.hv[at] - product[:, half * 128:half * 128 + 128]
        whole = pl.ds(part * step * 8, step * 8)
        if part < 2:
            @pl.when(c.row < 2)
            def _():
                c.hv[whole, :] = jnp.zeros((step * 8, 128), F)
        for p in range(2):
            @pl.when(c.col == p)
            def _(p=p):
                for ct in range(2):
                    c.hv[pl.ds(part * step * 8 + ct * 4, step, stride=8), :] = pr[p, rows, ct * 128:ct * 128 + 128]
        pltpu.make_async_copy(c.hv.at[whole], out.at[whole], c.sems["local"].at[part]).start()
    for part in range(4):
        whole = pl.ds(part * step * 8, step * 8)
        pltpu.make_async_copy(c.hv.at[whole], out.at[whole], c.sems["local"].at[part]).wait()


def kernel(dims, h, out, hv, rsrc, cbuf, rbuf, vbuf, dbuf, s, pr, rcat, ccat, *sems):
    c = Comm(*dims, h, hv, rsrc, cbuf, rbuf, vbuf, dbuf, dict(zip(NAMES, sems)))
    load = pltpu.make_async_copy(h, hv, c.sems["local"].at[3])
    load.start()
    c.barrier()
    load.wait()
    c.prepare()
    c.d_send()
    c.scatter_c()
    c.scatter_r()
    slots = c.slots()

    @pl.when(c.root)
    def _():
        factor(c, s, lambda j: c.slot(j) if j < slots else None)

    @pl.when(jnp.logical_not(c.root))
    def _():
        for j in range(8):
            if j < slots:
                c.slot(j)
            c.v_send(j, True)

    for p in range(2):
        panel_rows(c, p, pr, rcat)
        panel_columns(c, p, ccat)
    update(c, out, pr, rcat, ccat)
    c.finish()


def on_device(dims, hessian):
    i, r, l, w = hessian.shape
    nx, ny, nz = dims
    n = nx * ny
    flat = hessian.reshape(i, r, l, 2, 128).transpose(0, 1, 3, 2, 4).reshape(i * r * 2 * l, 128)
    out = pl.pallas_call(
        functools.partial(kernel, dims),
        out_shape=jax.ShapeDtypeStruct(flat.shape, F),
        in_specs=[pl.BlockSpec(memory_space=pl.ANY)],
        out_specs=pl.BlockSpec(memory_space=pl.ANY),
        scratch_shapes=[
            pltpu.VMEM(flat.shape, F),
            pltpu.VMEM((nz, 2, 2 * W // nz, 128), F),
            pltpu.VMEM((2, nx, ny, W * 8 // n, 128), F),
            pltpu.VMEM((2, nz, 2, 2 * W // nz, 128), F),
            pltpu.VMEM((8, 2, 64, W), F),
            pltpu.VMEM((2, 4, 2, 64, 128), F),
            pltpu.VMEM((W, 3 * W), F),
            pltpu.VMEM((2, 2 * W, W), F),
            pltpu.VMEM((2 * W, 6 * W), jnp.bfloat16),
            pltpu.VMEM((6 * W, 4 * W), jnp.bfloat16),
        ] + semaphores(nx, ny, nz),
        compiler_params=pltpu.CompilerParams(collective_id=0, has_side_effects=True, vmem_limit_bytes=40 << 20),
        name="panels",
    )(flat)
    return out.reshape(i, r, 2, l, 128).transpose(0, 1, 3, 2, 4).reshape(i, r, l, w)


def solution(mesh):
    spec = P(None, "row", None, "col")
    return jax.shard_map(
        functools.partial(on_device, (4, 8, 8)), mesh=mesh, in_specs=(spec,), out_specs=spec, check_vma=False
    )
```

time: 1030 us -> 104 us (0.10)
  the two profiles are of different devices: /device:TPU:64 before, /device:TPU:293 now
where the time goes in v1:
time: 104 us
  Pallas kernels  101 us (97%)
  local copies, waits for them, and re-layouts  2.91 us (3%)
    pallas_call x1, Pallas kernels, on_device(): pl.pallas_call(functools.partial(kernel, dims), out_shape=jax.ShapeDtypeS...  101 us
    unnamed x3, local copies, waits for them, and re-layouts  2.91 us

profile of v1, /device:TPU:293, one launch (start us, length us, event | category | flops | bytes accessed | tf_op | source)
XLA Modules:
  0.0 104.2 jit_solution(9819813235162340253)
XLA Ops:
  0.0 0.0 copy-start
  0.0 1.6 %copy-done = f32[2,256,4,256]{3,2,1,0:T(4,128)S(1)} copy-done((f32[2,256,4,256]{3,2,1,0:T(4,128)S(1)}, f32[2,256,4,256]{3,2,1,0:T(4,128)}, u32[]{:S(2)}) %copy-start) | copy-done | bytes 2097176
  1.6 101.2 %panels.1 = f32[4096,128]{1,0:T(8,128)S(1)} custom-call(f32[4096,128]{1,0:T(8,128)S(1)} %bitcast.11), custom_call_target="tpu_custom_call" | custom-call | tf_op jit(solution)/shard_map/panels/pallas_call | solution.py:537
  102.8 1.3 %copy.5 = f32[2,256,4,256]{3,2,1,0:T(4,128)} copy(f32[2,256,4,256]{3,2,1,0:T(4,128)S(1)} %bitcast.10) | data formatting | bytes 4194304
Async XLA Ops:
  0.0 1.6 %copy-start = (f32[2,256,4,256]{3,2,1,0:T(4,128)S(1)}, f32[2,256,4,256]{3,2,1,0:T(4,128)}, u32[]{:S(2)}) copy-start(f32[2,256,4,256]{3,2,1,0:T(4,128)} %param.1) | copy-start | bytes 6291460

commit v2 on v1

--- a/solution.py
+++ b/solution.py
@@ -11,6 +11,11 @@
 HI = lax.Precision.HIGHEST
 MESH = pl.DeviceIdType.MESH
 W = 256
+SUB = 2
+LAG = 1
+ROOT_LAG = 3
+LEAVES = (3, 5, 6, 7)
+RELAY = {1: (0, 2, 3, 4), 2: (1, 3, 4, 5), 3: (2, 4, 5, 6), 4: (3, 5, 6, 7)}
 
 
 def recip(p):
@@ -46,10 +51,10 @@
     return out
 
 class Comm:
-    def __init__(self, nx, ny, nz, h, hv, rsrc, cbuf, rbuf, vbuf, dbuf, sems):
+    def __init__(self, nx, ny, nz, h, hv, rsrc, cbuf, rbuf, vbuf, dbuf, via, sems):
         self.nx, self.ny, self.nz = nx, ny, nz
         self.h, self.hv, self.rsrc, self.cbuf, self.rbuf = h, hv, rsrc, cbuf, rbuf
-        self.vbuf, self.dbuf = vbuf, dbuf
+        self.vbuf, self.dbuf, self.via = vbuf, dbuf, via
         self.sems = sems
         self.row = lax.axis_index("row")
         self.col = lax.axis_index("col")
@@ -64,7 +69,7 @@
         k = self.k if k is None else k
         return (x * self.ny + y, z * 2 + k)
 
-    def barrier(self):
+    def signal(self):
         nx, ny, nz = self.nx, self.ny, self.nz
         sem = pltpu.get_barrier_semaphore()
 
@@ -73,75 +78,126 @@
 
         for root in range(2):
             pl.when(self.row != root)(lambda root=root: tell((root, self.col)))
-        pl.when(self.z != 0)(lambda: tell(self.at(z=0)))
+        for y in range(2):
+            pl.when(jnp.logical_and(self.x != 0, self.y != y))(lambda y=y: tell(self.at(y=y)))
         tell(self.at(k=1 - self.k))
         for d in (1, -1):
             tell(self.at(y=(self.y + d) % ny))
+        for d in range(1, nz):
             tell(self.at(z=(self.z + d) % nz))
         for d in range(1, nx):
             tell(self.at(x=(self.x + d) % nx))
         pl.when(self.root)(lambda: tell((1, 1)))
+
+    def barrier(self):
+        nx, ny, nz = self.nx, self.ny, self.nz
         total = 5 + nx - 1
         total = total + jnp.where(self.row < 2, nx * ny - 1, 0) + jnp.where(self.z == 0, nz - 1, 0)
         total = total + jnp.where(self.d_source(1), 1, 0)
-        pl.semaphore_wait(sem, total)
+        total = total + jnp.where(jnp.logical_and(self.x != 0, self.y < 2), ny - 1, 0)
+        total = total + nz - 3 - jnp.where(self.z == 0, nz - 1, 0)
+        pl.semaphore_wait(pltpu.get_barrier_semaphore(), total)
 
     def remote(self, src, dst, send, recv, device):
         return pltpu.make_async_remote_copy(
             src_ref=src, dst_ref=dst, send_sem=send, recv_sem=recv, device_id=device, device_id_type=MESH
         )
 
+    def piece_copy(self, root, u, p):
+        size = self.cbuf.shape[3] // SUB
+        return self.remote(
+            self.h.at[pl.ds((p * SUB + u) * size, size)],
+            self.cbuf.at[root, p // self.ny, p % self.ny, pl.ds(u * size, size)],
+            self.sems["cs_send"].at[u, p], self.sems["cs_recv"].at[u, root], (p, self.col),
+        )
+
+    def own_piece(self, root):
+        size = self.cbuf.shape[3]
+        return pltpu.make_async_copy(
+            self.h.at[pl.ds(root * size, size)], self.cbuf.at[root, 0, root], self.sems["local"].at[root]
+        )
+
+    def via_copy(self, root, p):
+        size = self.cbuf.shape[3] // SUB
+        return self.remote(
+            self.h.at[pl.ds((p * SUB + 1) * size, size)], self.via.at[p % self.ny],
+            self.sems["cs_send"].at[1, p], self.sems["cv_recv"].at[p % self.ny], ((p // self.ny) * self.ny + root, self.col),
+        )
+
+    def on_copy(self, root, y):
+        size = self.cbuf.shape[3] // SUB
+        return self.remote(
+            self.via.at[y], self.cbuf.at[root, self.x, y, pl.ds(size, size)],
+            self.sems["cs_send"].at[1, y], self.sems["cs_recv"].at[1, root], self.at(y=y))
+
+    def on_own(self, root):
+        size = self.cbuf.shape[3] // SUB
+        return pltpu.make_async_copy(
+            self.via.at[root], self.cbuf.at[root, self.x, root, pl.ds(size, size)], self.sems["local"].at[4])
+
     def scatter_c(self):
         nx, ny = self.nx, self.ny
-        n = nx * ny
-        sems_s, sems_r, local = self.sems["cs_send"], self.sems["cs_recv"], self.sems["local"]
-        size = self.cbuf.shape[3]
         for root in range(2):
 
             @pl.when(self.row == root)
             def _(root=root):
+                self.own_piece(root).start()
+
                 def send(i, carry):
                     p = (i % nx) * ny + (i // nx + root) % ny
-                    copy = self.remote(
-                        self.h.at[pl.ds(p * size, size)],
-                        self.cbuf.at[root, p // ny, p % ny],
-                        sems_s.at[p], sems_r.at[root], (p, self.col),
-                    )
-                    pl.when(p != root)(copy.start)
+                    pl.when(p != root)(self.piece_copy(root, 0, p).start)
+                    pl.when(p >= ny)(self.via_copy(root, p).start)
+                    pl.when(jnp.logical_and(p < ny, p != root))(self.piece_copy(root, 1, p).start)
                     return carry
-                lax.fori_loop(0, n, send, 0)
-                pltpu.make_async_copy(
-                    self.h.at[pl.ds(root * size, size)], self.cbuf.at[root, 0, root], local.at[root]
-                ).start()
-
-    def scatter_c_wait(self, root):
-        size = self.cbuf.shape[3]
-
-        @pl.when(self.row == root)
-        def _():
-            pltpu.make_async_copy(
-                self.h.at[pl.ds(root * size, size)], self.cbuf.at[root, 0, root], self.sems["local"].at[root]
-            ).wait()
-
-        @pl.when(self.row != root)
-        def _():
-            piece = self.cbuf.at[root, self.x, self.y]
-            self.remote(piece, piece, self.sems["cs_send"].at[0], self.sems["cs_recv"].at[root], self.at()).wait_recv()
+                lax.fori_loop(0, nx * ny, send, 0)
+
+    def relays(self, root):
+        return jnp.logical_and(self.x != 0, self.y == root)
+
+    def hand_on(self):
+        for root in range(2):
+
+            @pl.when(self.relays(root))
+            def _(root=root):
+                def step(i, carry):
+                    y = (i + root) % self.ny
+                    self.via_copy(root, self.x * self.ny + y).wait_recv()
+                    pl.when(y != root)(self.on_copy(root, y).start)
+                    pl.when(y == root)(self.on_own(root).start)
+                    return carry
+                lax.fori_loop(0, self.ny, step, 0)
+
+    def scatter_c_wait(self, root, u):
+        size = self.cbuf.shape[3] // SUB
+        if u == 0:
+            pl.when(self.row == root)(lambda: self.own_piece(root).wait())
+        waits = self.row != root
+        if u == 1:
+            waits = jnp.logical_and(waits, jnp.logical_not(self.relays(root)))
+            pl.when(self.relays(root))(lambda: self.on_own(root).wait())
+
+        @pl.when(waits)
+        def _():
+            piece = self.cbuf.at[root, self.x, self.y, pl.ds(u * size, size)]
+            self.remote(piece, piece, self.sems["cs_send"].at[u, 0], self.sems["cs_recv"].at[u, root], self.at()).wait_recv()
 
     def scatter_c_done(self):
-        size = self.cbuf.shape[3]
         for root in range(2):
 
             @pl.when(self.row == root)
             def _(root=root):
-                def done(p, carry):
-                    copy = self.remote(
-                        self.h.at[pl.ds(p * size, size)], self.cbuf.at[root, p // self.ny, p % self.ny],
-                        self.sems["cs_send"].at[p], self.sems["cs_recv"].at[root], (p, self.col),
-                    )
-                    pl.when(p != root)(copy.wait_send)
+                for u in range(SUB):
+                    def done(p, carry, u=u):
+                        pl.when(p != root)(self.piece_copy(root, u, p).wait_send)
+                        return carry
+                    lax.fori_loop(0, self.nx * self.ny, done, 0)
+
+            @pl.when(self.relays(root))
+            def _(root=root):
+                def done_on(y, carry):
+                    pl.when(y != root)(self.on_copy(root, y).wait_send)
                     return carry
-                lax.fori_loop(0, self.nx * self.ny, done, 0)
+                lax.fori_loop(0, self.ny, done_on, 0)
 
     def scatter_r_copy(self, q):
         return self.remote(
@@ -184,8 +240,8 @@
         for way, sign in enumerate((1, -1)):
             index = (me - sign * (step - 1)) % n
             ref = piece(index, way if step == half else None)
-            send = self.sems[name].at[0, way, step - 1]
-            recv = self.sems[name].at[1, way, step - 1]
+            send = self.sems[name[0]].at[name[1], 0, way, step - 1]
+            recv = self.sems[name[0]].at[name[1], 1, way, step - 1]
             out.append(self.remote(ref, ref, send, recv, device((me + sign) % n)))
         return out
 
@@ -198,8 +254,8 @@
         for way, sign in enumerate((1, -1)):
             index = (me - sign * step) % n
             ref = piece(index, way if step == half else None)
-            send = self.sems[name].at[0, way, step - 1]
-            recv = self.sems[name].at[1, way, step - 1]
+            send = self.sems[name[0]].at[name[1], 0, way, step - 1]
+            recv = self.sems[name[0]].at[name[1], 1, way, step - 1]
             self.remote(ref, ref, send, recv, device((me + sign) % n)).wait_recv()
 
     def ring_done(self, name, *args):
@@ -208,42 +264,22 @@
 
     def rings(self):
         c = self.cbuf
-        hs = c.shape[3] // 2
-        hr = self.rbuf.shape[3] // 2
-
-        def px0(i, h):
-            ref = c.at[0, i, self.y]
-            return ref if h is None else ref.at[pl.ds(h * hs, hs)]
-
-        def py0(i, h):
-            if h is None:
-                return c.at[0, :, i]
-            return c.at[0, :, i, pl.ds(h * hs, hs)]
-
-        def py1(i, h):
-            ref = c.at[1, self.x, i]
-            return ref if h is None else ref.at[pl.ds(h * hs, hs)]
-
-        def px1(i, h):
-            if h is None:
-                return c.at[1, i]
-            return c.at[1, i, pl.ds(h * (self.ny // 2), self.ny // 2)]
-
-        def pz(i, h):
-            if h is None:
-                return self.rbuf.at[self.k, i]
-            return self.rbuf.at[self.k, i, h]
-
-        dx = lambda i: self.at(x=i)
-        dy = lambda i: self.at(y=i)
-        dz = lambda i: self.at(z=i)
-        return {
-            "x0": ("x0", self.nx, self.x, dx, px0),
-            "y0": ("y0", self.ny, self.y, dy, py0),
-            "y1": ("y1", self.ny, self.y, dy, py1),
-            "x1": ("x1", self.nx, self.x, dx, px1),
-            "z": ("z", self.nz, self.z, dz, pz),
-        }
+        size = c.shape[3] // SUB
+        hy = self.ny // 2
+
+        def part(u, h):
+            return pl.ds(u * size, size) if h is None else pl.ds(u * size + h * (size // 2), size // 2)
+
+        out = {}
+        for u in range(SUB):
+            out["x0", u] = (self.nx, self.x, lambda i: self.at(x=i), lambda i, h, u=u: c.at[0, i, self.y, part(u, h)])
+            out["y0", u] = (self.ny, self.y, lambda i: self.at(y=i), lambda i, h, u=u: c.at[0, :, i, part(u, h)])
+            out["y1", u] = (self.ny, self.y, lambda i: self.at(y=i), lambda i, h, u=u: c.at[1, self.x, i, part(u, h)])
+            out["x1", u] = (self.nx, self.x, lambda i: self.at(x=i), lambda i, h, u=u: c.at[
+                1, i, slice(None) if h is None else pl.ds(h * hy, hy), part(u, None)])
+        out["z", 0] = (self.nz, self.z, lambda i: self.at(z=i), lambda i, h: (
+            self.rbuf.at[self.k, i] if h is None else self.rbuf.at[self.k, i, h]))
+        return {key: (key,) + value for key, value in out.items()}
 
     def swap_copy(self, kk):
         return self.remote(
@@ -286,87 +322,129 @@
         for b in range(2):
             pl.when(self.d_source(b))(lambda b=b: self.d_copy(b).wait_send())
 
-    def v_stages(self, j):
-        chunk = self.vbuf.at[j, 0] if j < 4 else self.vbuf.at[j]
-        send, recv = self.sems["v_send"], self.sems["v_recv"].at[j]
+    def v_part(self, b, i):
+        if b == 0:
+            return self.vbuf.at[i // 2, 0, pl.ds(pl.multiple_of((i % 2) * 32, 32), 32)]
+        if b == 1:
+            return self.vbuf.at[4 + i // 4, :, pl.ds(pl.multiple_of((i % 4) * 16, 16), 16)]
+        return self.vbuf.at[4 + b, :, pl.ds(pl.multiple_of(i * 8, 8), 8)]
+
+    def v_whole(self, b):
+        return (self.vbuf.at[pl.ds(0, 4), 0], self.vbuf.at[pl.ds(4, 2)], self.vbuf.at[6], self.vbuf.at[7])[b]
+
+    def v_plan(self, b):
+        nx, ny, nz = self.nx, self.ny, self.nz
+        send, recv = self.sems["v_send"], self.sems["v_recv"]
         first = self.k == 0
         on_x = jnp.logical_and(first, self.x == 0)
-        on_z = jnp.logical_and(on_x, self.z == 0)
-        plan, base = [], 0
-        for on, n, place in (
-            (self.root, self.ny, lambda d: self.at(y=d)),
-            (on_z, self.nz, lambda d: self.at(z=d)),
-            (on_x, self.nx, lambda d: self.at(x=d)),
-            (first, 2, lambda d: self.at(k=d)),
-        ):
-            plan.append((on, [functools.partial(self.remote, chunk, chunk, send.at[j, base + d - 1], recv, place(d)) for d in range(1, n)]))
-            base += n - 1
+        on_y = jnp.logical_and(on_x, self.y == 0)
+
+        def copy(i, slot, device):
+            part = self.v_part(b, i)
+            return functools.partial(self.remote, part, part, send.at[b, slot], recv.at[b, i], device)
+
+        plan = [(self.root, copy(d, d - 1, self.at(z=d))) for d in range(1, nz)]
+        base = nz - 2
+        plan += [(on_y, copy(self.z, base + d, self.at(y=d))) for d in range(1, ny)]
+        base += ny - 1
+        plan += [(on_x, copy(self.z, base + d, self.at(x=d))) for d in range(1, nx)]
+        base += nx - 1
+        for d in range(1, nz):
+            z = (self.z + d) % nz
+            to = jnp.logical_and(first, jnp.logical_or(self.row != 0, z != 0))
+            plan.append((to, copy(self.z, base + d, self.at(z=z))))
         return plan
 
-    def v_wait(self, j):
-        plan = self.v_stages(j)
-        pl.when(jnp.logical_not(self.root))(lambda: plan[3][1][0]().wait_recv())
-
-    def v_send(self, j, wait):
-        if wait:
-            self.v_wait(j)
-        for on, copies in self.v_stages(j):
-            @pl.when(on)
-            def _(copies=copies):
-                for copy in copies:
-                    copy().start()
-
-    def v_done(self, j):
-        for on, copies in self.v_stages(j):
-            @pl.when(on)
-            def _(copies=copies):
-                for copy in copies:
-                    copy().wait_send()
+    def v_swap(self, b):
+        whole = self.v_whole(b)
+        return self.remote(whole, whole, self.sems["v_swap"].at[0, b], self.sems["v_swap"].at[1, b], self.at(k=1 - self.k))
+
+    def v_relay(self, b):
+        part = self.v_part(b, self.z)
+
+        @pl.when(jnp.logical_and(self.k == 0, jnp.logical_not(self.root)))
+        def _():
+            self.remote(part, part, self.sems["v_send"].at[b, 0], self.sems["v_recv"].at[b, self.z], self.at()).wait_recv()
+
+        for on, copy in self.v_plan(b):
+            pl.when(on)(lambda copy=copy: copy().start())
+
+    def v_collect(self, b):
+        @pl.when(self.k == 0)
+        def _():
+            @pl.when(jnp.logical_not(self.root))
+            def _():
+                for d in range(1, self.nz):
+                    z = (self.z + d) % self.nz
+                    part = self.v_part(b, z)
+                    self.remote(part, part, self.sems["v_send"].at[b, 0], self.sems["v_recv"].at[b, z], self.at()).wait_recv()
+            self.v_swap(b).start()
+
+    def v_wait(self, b):
+        pl.when(self.k == 1)(lambda: self.v_swap(b).wait_recv())
+
+    def v_done(self, b):
+        for on, copy in self.v_plan(b):
+            pl.when(on)(lambda copy=copy: copy().wait_send())
+        pl.when(self.k == 0)(lambda: self.v_swap(b).wait_send())
+
+    def depth(self, d):
+        on_x = self.x == 0
+        on_y = jnp.logical_and(on_x, self.y == 0)
+        return jnp.logical_and(self.k == 0, (
+            None, jnp.logical_and(on_y, self.z != 0), jnp.logical_and(on_x, self.y != 0), self.x != 0)[d])
 
     def sequences(self):
         steps = {"x": self.nx // 2, "y": self.ny // 2, "z": self.nz // 2}
-        names = (("x0", "y0"), ("y1", "x1"), ("z",))
-        return [[(n, t) for n in chain for t in range(1, steps[n[0]] + 1)] for chain in names]
-
-    def slot(self, s):
+        chains = []
+        for u in range(SUB):
+            for root, names in enumerate((("x0", "y0"), ("y1", "x1"))):
+                first = functools.partial(self.scatter_c_wait, root, u)
+                chains.append((u * LAG, first, [((n, u), t) for n in names for t in range(1, steps[n[0]] + 1)]))
+        chains.append((0, self.scatter_r_wait, [(("z", 0), t) for t in range(1, steps["z"] + 1)]))
+        return chains
+
+    def slot(self, slot):
         r = self.rings()
-        for i, chain in enumerate(self.sequences()):
+        for begin, first, chain in self.sequences():
+            s = slot - begin
             if s == 0:
-                (self.scatter_r_wait if i == 2 else functools.partial(self.scatter_c_wait, i))()
-            elif s <= len(chain):
+                first()
+            elif 0 < s <= len(chain):
                 self.ring_wait(*r[chain[s - 1][0]], chain[s - 1][1])
-            if s < len(chain):
+            if 0 <= s < len(chain):
                 self.ring_start(*r[chain[s][0]], chain[s][1])
-            if i == 2 and s == len(chain):
+            if s == len(chain) and chain[0][0][0] == "z":
                 self.swap_start()
-        if s == self.slots() - 1:
+        if slot == self.slots() - 1:
             self.swap_wait()
 
     def slots(self):
-        return 1 + max(len(chain) for chain in self.sequences())
+        return 1 + max(begin + len(chain) for begin, _, chain in self.sequences())
 
     def finish(self):
         r = self.rings()
-        for chain in self.sequences():
+        for _, _, chain in self.sequences():
             for name, step in chain:
                 self.ring_done(*r[name], step)
         self.scatter_c_done()
         self.scatter_r_done()
         self.swap_done()
         self.d_done()
-        for j in range(8):
-            self.v_done(j)
-
-
-NAMES = ("local", "cs_send", "cs_recv", "rs_send", "rs_recv", "x0", "y0", "y1", "x1", "z", "swap", "d", "v_send", "v_recv")
+        for b in range(4):
+            self.v_done(b)
+
+
+NAMES = ("local", "cs_send", "cs_recv", "rs_send", "rs_recv", "x0", "y0", "y1", "x1", "z", "swap", "d", "v_send", "v_recv", "v_swap", "cv_recv")
 
 
 def semaphores(nx, ny, nz):
     dma = pltpu.SemaphoreType.DMA
     shapes = {
-        "local": (6,), "cs_send": (nx * ny,), "cs_recv": (2,), "rs_send": (nz,), "rs_recv": (),
-        "x0": (2, 2, nx // 2), "y0": (2, 2, ny // 2), "y1": (2, 2, ny // 2), "x1": (2, 2, nx // 2),
-        "z": (2, 2, nz // 2), "swap": (2,), "d": (3,), "v_send": (8, nx + ny + nz - 2), "v_recv": (8,),
+        "local": (6,), "cs_send": (SUB, nx * ny), "cs_recv": (SUB, 2), "rs_send": (nz,), "rs_recv": (),
+        "x0": (SUB, 2, 2, nx // 2), "y0": (SUB, 2, 2, ny // 2), "y1": (SUB, 2, 2, ny // 2), "x1": (SUB, 2, 2, nx // 2),
+        "z": (1, 2, 2, nz // 2), "swap": (2,), "d": (3,), "v_send": (4, nx + ny + 2 * nz - 4), "v_recv": (4, nz), "v_swap": (2, 4),
+        "cv_recv": (ny,),
     }
     return [dma(shapes[name]) for name in NAMES]
 
@@ -392,7 +470,7 @@
     return jnp.concatenate([ref[:, ct].reshape(q * rows, 128) for ct in range(2)], axis=1)
 
 
-def factor(c, s, hook):
+def factor(c, s, begin, hook):
     vbuf = c.vbuf
     s[:, 0:W] = eye(W)
     s[:, W:2 * W] = jnp.zeros((W, W), F)
@@ -416,7 +494,11 @@
             vbuf[j, 0] = r[:, 0:W]
             if p == 1:
                 vbuf[j, 1] = r[:, W:2 * W]
-            c.v_send(j, False)
+            if j == 0:
+                begin()
+            if j in LEAVES:
+                c.v_relay(LEAVES.index(j))
+                c.v_collect(LEAVES.index(j))
             if i < 3:
                 col = dot_t(s[hi:W, 2 * W + lo:2 * W + hi], w)
                 s[hi:W, :] = s[hi:W, :] - dot(col, r)
@@ -499,28 +581,46 @@
         pltpu.make_async_copy(c.hv.at[whole], out.at[whole], c.sems["local"].at[part]).wait()
 
 
-def kernel(dims, h, out, hv, rsrc, cbuf, rbuf, vbuf, dbuf, s, pr, rcat, ccat, *sems):
-    c = Comm(*dims, h, hv, rsrc, cbuf, rbuf, vbuf, dbuf, dict(zip(NAMES, sems)))
+def kernel(dims, h, out, hv, rsrc, cbuf, rbuf, vbuf, dbuf, via, s, pr, rcat, ccat, *sems):
+    c = Comm(*dims, h, hv, rsrc, cbuf, rbuf, vbuf, dbuf, via, dict(zip(NAMES, sems)))
     load = pltpu.make_async_copy(h, hv, c.sems["local"].at[3])
     load.start()
-    c.barrier()
+    c.signal()
     load.wait()
     c.prepare()
-    c.d_send()
-    c.scatter_c()
-    c.scatter_r()
+
+    def begin():
+        c.barrier()
+        c.d_send()
+        c.scatter_c()
+        c.scatter_r()
+        c.hand_on()
+
     slots = c.slots()
 
     @pl.when(c.root)
     def _():
-        factor(c, s, lambda j: c.slot(j) if j < slots else None)
+        def hook(j):
+            if j >= ROOT_LAG:
+                c.slot(j - ROOT_LAG)
+        factor(c, s, begin, hook)
+        for t in range(8 - ROOT_LAG, slots):
+            c.slot(t)
 
     @pl.when(jnp.logical_not(c.root))
     def _():
-        for j in range(8):
-            if j < slots:
-                c.slot(j)
-            c.v_send(j, True)
+        begin()
+        for t in range(slots):
+            c.slot(t)
+            for depth in (1, 2, 3):
+                for b in range(4):
+                    if RELAY[depth][b] == t:
+                        pl.when(c.depth(depth))(lambda b=b: c.v_relay(b))
+            for b in range(4):
+                if RELAY[4][b] == t:
+                    c.v_collect(b)
+        for b in range(4):
+            c.v_wait(b)
 
     for p in range(2):
         panel_rows(c, p, pr, rcat)
@@ -537,7 +637,7 @@
     out = pl.pallas_call(
         functools.partial(kernel, dims),
         out_shape=jax.ShapeDtypeStruct(flat.shape, F),
-        in_specs=[pl.BlockSpec(memory_space=pl.ANY)],
+        in_specs=[pl.BlockSpec(memory_space=pltpu.HBM)],
         out_specs=pl.BlockSpec(memory_space=pl.ANY),
         scratch_shapes=[
             pltpu.VMEM(flat.shape, F),
@@ -546,6 +646,7 @@
             pltpu.VMEM((2, nz, 2, 2 * W // nz, 128), F),
             pltpu.VMEM((8, 2, 64, W), F),
             pltpu.VMEM((2, 4, 2, 64, 128), F),
+            pltpu.VMEM((ny, W * 8 // n // SUB, 128), F),
             pltpu.VMEM((W, 3 * W), F),
             pltpu.VMEM((2, 2 * W, W), F),
             pltpu.VMEM((2 * W, 6 * W), jnp.bfloat16),

time: 104 us -> 78.2 us (0.75)
  the two profiles are of different devices: /device:TPU:293 before, /device:TPU:37 now
where the time goes in v2:
time: 78.2 us; the launch traced here: 78.1 us
  Pallas kernels  75.2 us (96%)
  local copies, waits for them, and re-layouts  2.91 us (4%)
    pallas_call x1, Pallas kernels, on_device(): pl.pallas_call(functools.partial(kernel, dims), out_shape=jax.ShapeDtypeS...  75.2 us
    unnamed x3, local copies, waits for them, and re-layouts  2.91 us

profile of v2, /device:TPU:37, one launch (start us, length us, event | category | flops | bytes accessed | tf_op | source)
XLA Modules:
  0.0 78.1 jit_solution(1763563349015594629)
XLA Ops:
  0.0 0.0 copy-start
  0.0 1.6 %copy-done = f32[2,256,4,256]{3,2,1,0:T(4,128)S(1)} copy-done((f32[2,256,4,256]{3,2,1,0:T(4,128)S(1)}, f32[2,256,4,256]{3,2,1,0:T(4,128)}, u32[]{:S(2)}) %copy-start) | copy-done | bytes 2097176
  1.6 75.2 %panels.1 = f32[4096,128]{1,0:T(8,128)S(1)} custom-call(f32[4096,128]{1,0:T(8,128)S(1)} %bitcast.11), custom_call_target="tpu_custom_call" | custom-call | tf_op jit(solution)/shard_map/panels/pallas_call | solution.py:637
  76.8 1.3 %copy.5 = f32[2,256,4,256]{3,2,1,0:T(4,128)} copy(f32[2,256,4,256]{3,2,1,0:T(4,128)S(1)} %bitcast.10) | data formatting | bytes 4194304
Async XLA Ops:
  0.0 1.6 %copy-start = (f32[2,256,4,256]{3,2,1,0:T(4,128)S(1)}, f32[2,256,4,256]{3,2,1,0:T(4,128)}, u32[]{:S(2)}) copy-start(f32[2,256,4,256]{3,2,1,0:T(4,128)} %param.1) | copy-start | bytes 6291460

commit v3 on v2

--- a/solution.py
+++ b/solution.py
@@ -12,10 +12,9 @@
 MESH = pl.DeviceIdType.MESH
 W = 256
 SUB = 2
-LAG = 1
-ROOT_LAG = 3
+ROOT = {4: (0,), 6: (1,), 7: (2,)}
 LEAVES = (3, 5, 6, 7)
-RELAY = {1: (0, 2, 3, 4), 2: (1, 3, 4, 5), 3: (2, 4, 5, 6), 4: (3, 5, 6, 7)}
+RELAY = {1: (0, 1, 2, 3), 2: (1, 2, 3, 4), 3: (2, 3, 4, 5), 4: (3, 4, 5, 9)}
 
 
 def recip(p):
@@ -78,24 +77,20 @@
 
         for root in range(2):
             pl.when(self.row != root)(lambda root=root: tell((root, self.col)))
-        for y in range(2):
-            pl.when(jnp.logical_and(self.x != 0, self.y != y))(lambda y=y: tell(self.at(y=y)))
         tell(self.at(k=1 - self.k))
-        for d in (1, -1):
+        for d in range(1, ny):
             tell(self.at(y=(self.y + d) % ny))
         for d in range(1, nz):
             tell(self.at(z=(self.z + d) % nz))
         for d in range(1, nx):
             tell(self.at(x=(self.x + d) % nx))
         pl.when(self.root)(lambda: tell((1, 1)))
+        pl.when(jnp.logical_and(jnp.logical_and(self.row == 0, self.k == 1), self.z != 0))(lambda: tell((0, 0)))
 
     def barrier(self):
         nx, ny, nz = self.nx, self.ny, self.nz
-        total = 5 + nx - 1
-        total = total + jnp.where(self.row < 2, nx * ny - 1, 0) + jnp.where(self.z == 0, nz - 1, 0)
-        total = total + jnp.where(self.d_source(1), 1, 0)
-        total = total + jnp.where(jnp.logical_and(self.x != 0, self.y < 2), ny - 1, 0)
-        total = total + nz - 3 - jnp.where(self.z == 0, nz - 1, 0)
+        total = nx + ny + nz - 2 + jnp.where(self.row < 2, nx * ny - 1, 0) + jnp.where(self.d_source(1), 1, 0)
+        total = total + jnp.where(self.root, nz - 1, 0)
         pl.semaphore_wait(pltpu.get_barrier_semaphore(), total)
 
     def remote(self, src, dst, send, recv, device):
@@ -240,8 +235,8 @@
         for way, sign in enumerate((1, -1)):
             index = (me - sign * (step - 1)) % n
             ref = piece(index, way if step == half else None)
-            send = self.sems[name[0]].at[name[1], 0, way, step - 1]
-            recv = self.sems[name[0]].at[name[1], 1, way, step - 1]
+            send = self.sems[name].at[0, way, step - 1]
+            recv = self.sems[name].at[1, way, step - 1]
             out.append(self.remote(ref, ref, send, recv, device((me + sign) % n)))
         return out
 
@@ -254,31 +249,45 @@
         for way, sign in enumerate((1, -1)):
             index = (me - sign * step) % n
             ref = piece(index, way if step == half else None)
-            send = self.sems[name[0]].at[name[1], 0, way, step - 1]
-            recv = self.sems[name[0]].at[name[1], 1, way, step - 1]
+            send = self.sems[name].at[0, way, step - 1]
+            recv = self.sems[name].at[1, way, step - 1]
             self.remote(ref, ref, send, recv, device((me + sign) % n)).wait_recv()
 
     def ring_done(self, name, *args):
         for copy in self.ring(name, *args):
             copy.wait_send()
 
+    def direct(self, name, n, me, device, piece, d):
+        ref = piece(me, None)
+        return self.remote(ref, ref, self.sems[name].at[0, d], self.sems[name].at[1, d], device((me + d) % n))
+
+    def direct_start(self, name, n, *args):
+        for d in range(1, n):
+            self.direct(name, n, *args, d).start()
+
+    def direct_wait(self, name, n, me, device, piece):
+        for d in range(1, n):
+            ref = piece((me - d) % n, None)
+            self.remote(ref, ref, self.sems[name].at[0, d], self.sems[name].at[1, d], device((me + d) % n)).wait_recv()
+
+    def direct_done(self, name, n, *args):
+        for d in range(1, n):
+            self.direct(name, n, *args, d).wait_send()
+
     def rings(self):
         c = self.cbuf
-        size = c.shape[3] // SUB
-        hy = self.ny // 2
-
-        def part(u, h):
-            return pl.ds(u * size, size) if h is None else pl.ds(u * size + h * (size // 2), size // 2)
-
-        out = {}
-        for u in range(SUB):
-            out["x0", u] = (self.nx, self.x, lambda i: self.at(x=i), lambda i, h, u=u: c.at[0, i, self.y, part(u, h)])
-            out["y0", u] = (self.ny, self.y, lambda i: self.at(y=i), lambda i, h, u=u: c.at[0, :, i, part(u, h)])
-            out["y1", u] = (self.ny, self.y, lambda i: self.at(y=i), lambda i, h, u=u: c.at[1, self.x, i, part(u, h)])
-            out["x1", u] = (self.nx, self.x, lambda i: self.at(x=i), lambda i, h, u=u: c.at[
-                1, i, slice(None) if h is None else pl.ds(h * hy, hy), part(u, None)])
-        out["z", 0] = (self.nz, self.z, lambda i: self.at(z=i), lambda i, h: (
-            self.rbuf.at[self.k, i] if h is None else self.rbuf.at[self.k, i, h]))
+        size, hy = c.shape[3] // 2, self.ny // 2
+
+        def part(h):
+            return slice(None) if h is None else pl.ds(h * size, size)
+
+        out = {
+            "x0": (self.nx, self.x, lambda i: self.at(x=i), lambda i, h: c.at[0, i, self.y]),
+            "y0": (self.ny, self.y, lambda i: self.at(y=i), lambda i, h: c.at[0, :, i, part(h)]),
+            "y1": (self.ny, self.y, lambda i: self.at(y=i), lambda i, h: c.at[1, self.x, i]),
+            "x1": (self.nx, self.x, lambda i: self.at(x=i), lambda i, h: c.at[1, i, slice(None) if h is None else pl.ds(h * hy, hy)]),
+            "z": (self.nz, self.z, lambda i: self.at(z=i), lambda i, h: self.rbuf.at[self.k, i]),
+        }
         return {key: (key,) + value for key, value in out.items()}
 
     def swap_copy(self, kk):
@@ -335,7 +344,8 @@
     def v_plan(self, b):
         nx, ny, nz = self.nx, self.ny, self.nz
         send, recv = self.sems["v_send"], self.sems["v_recv"]
-        first = self.k == 0
+        core = b % 2
+        first = self.k == core
         on_x = jnp.logical_and(first, self.x == 0)
         on_y = jnp.logical_and(on_x, self.y == 0)
 
@@ -343,15 +353,15 @@
             part = self.v_part(b, i)
             return functools.partial(self.remote, part, part, send.at[b, slot], recv.at[b, i], device)
 
-        plan = [(self.root, copy(d, d - 1, self.at(z=d))) for d in range(1, nz)]
-        base = nz - 2
+        plan = [(self.root, copy(d, d, self.at(z=d, k=core))) for d in range(1 - core, nz)]
+        base = nz - 1
         plan += [(on_y, copy(self.z, base + d, self.at(y=d))) for d in range(1, ny)]
         base += ny - 1
         plan += [(on_x, copy(self.z, base + d, self.at(x=d))) for d in range(1, nx)]
         base += nx - 1
         for d in range(1, nz):
             z = (self.z + d) % nz
-            to = jnp.logical_and(first, jnp.logical_or(self.row != 0, z != 0))
+            to = first if core else jnp.logical_and(first, jnp.logical_or(self.row != 0, z != 0))
             plan.append((to, copy(self.z, base + d, self.at(z=z))))
         return plan
 
@@ -359,10 +369,15 @@
         whole = self.v_whole(b)
         return self.remote(whole, whole, self.sems["v_swap"].at[0, b], self.sems["v_swap"].at[1, b], self.at(k=1 - self.k))
 
+    def v_swaps(self, b):
+        if b % 2 == 0:
+            return self.k == 0
+        return jnp.logical_and(self.k == 1, jnp.logical_or(self.row != 0, self.z != 0))
+
     def v_relay(self, b):
         part = self.v_part(b, self.z)
 
-        @pl.when(jnp.logical_and(self.k == 0, jnp.logical_not(self.root)))
+        @pl.when(jnp.logical_and(self.k == b % 2, jnp.logical_not(self.root)))
         def _():
             self.remote(part, part, self.sems["v_send"].at[b, 0], self.sems["v_recv"].at[b, self.z], self.at()).wait_recv()
 
@@ -370,63 +385,63 @@
             pl.when(on)(lambda copy=copy: copy().start())
 
     def v_collect(self, b):
-        @pl.when(self.k == 0)
-        def _():
-            @pl.when(jnp.logical_not(self.root))
-            def _():
-                for d in range(1, self.nz):
-                    z = (self.z + d) % self.nz
-                    part = self.v_part(b, z)
-                    self.remote(part, part, self.sems["v_send"].at[b, 0], self.sems["v_recv"].at[b, z], self.at()).wait_recv()
-            self.v_swap(b).start()
+        @pl.when(jnp.logical_and(self.k == b % 2, jnp.logical_not(self.root)))
+        def _():
+            for d in range(1, self.nz):
+                z = (self.z + d) % self.nz
+                part = self.v_part(b, z)
+                self.remote(part, part, self.sems["v_send"].at[b, 0], self.sems["v_recv"].at[b, z], self.at()).wait_recv()
+        pl.when(self.v_swaps(b))(lambda: self.v_swap(b).start())
 
     def v_wait(self, b):
-        pl.when(self.k == 1)(lambda: self.v_swap(b).wait_recv())
+        pl.when(jnp.logical_and(self.k != b % 2, jnp.logical_not(self.root)))(lambda: self.v_swap(b).wait_recv())
 
     def v_done(self, b):
         for on, copy in self.v_plan(b):
             pl.when(on)(lambda copy=copy: copy().wait_send())
-        pl.when(self.k == 0)(lambda: self.v_swap(b).wait_send())
-
-    def depth(self, d):
+        pl.when(self.v_swaps(b))(lambda: self.v_swap(b).wait_send())
+
+    def depth(self, d, b):
         on_x = self.x == 0
         on_y = jnp.logical_and(on_x, self.y == 0)
-        return jnp.logical_and(self.k == 0, (
-            None, jnp.logical_and(on_y, self.z != 0), jnp.logical_and(on_x, self.y != 0), self.x != 0)[d])
+        first = jnp.logical_and(on_y, self.z != 0) if b % 2 == 0 else on_y
+        return jnp.logical_and(self.k == b % 2, (None, first, jnp.logical_and(on_x, self.y != 0), self.x != 0)[d])
 
     def sequences(self):
-        steps = {"x": self.nx // 2, "y": self.ny // 2, "z": self.nz // 2}
-        chains = []
-        for u in range(SUB):
-            for root, names in enumerate((("x0", "y0"), ("y1", "x1"))):
-                first = functools.partial(self.scatter_c_wait, root, u)
-                chains.append((u * LAG, first, [((n, u), t) for n in names for t in range(1, steps[n[0]] + 1)]))
-        chains.append((0, self.scatter_r_wait, [(("z", 0), t) for t in range(1, steps["z"] + 1)]))
-        return chains
+        steps = {"x1": self.nx // 2, "y0": self.ny // 2}
+        return [[(one, 0)] + [(ring, t) for t in range(1, steps[ring] + 1)] for one, ring in (("x0", "y0"), ("y1", "x1"))]
 
     def slot(self, slot):
         r = self.rings()
-        for begin, first, chain in self.sequences():
-            s = slot - begin
-            if s == 0:
-                first()
-            elif 0 < s <= len(chain):
-                self.ring_wait(*r[chain[s - 1][0]], chain[s - 1][1])
-            if 0 <= s < len(chain):
-                self.ring_start(*r[chain[s][0]], chain[s][1])
-            if s == len(chain) and chain[0][0][0] == "z":
-                self.swap_start()
+        chains = self.sequences()
+        if slot == 0:
+            for root in range(2):
+                for u in range(SUB):
+                    self.scatter_c_wait(root, u)
+                self.direct_start(*r[chains[root][0][0]])
+            self.scatter_r_wait()
+            self.direct_start(*r["z"])
+        for chain in chains:
+            if 0 < slot <= len(chain):
+                name, step = chain[slot - 1]
+                self.direct_wait(*r[name]) if step == 0 else self.ring_wait(*r[name], step)
+            if 0 < slot < len(chain):
+                self.ring_start(*r[chain[slot][0]], chain[slot][1])
+        if slot == 2:
+            self.direct_wait(*r["z"])
+            self.swap_start()
         if slot == self.slots() - 1:
             self.swap_wait()
 
     def slots(self):
-        return 1 + max(begin + len(chain) for begin, _, chain in self.sequences())
+        return 1 + max(len(chain) for chain in self.sequences())
 
     def finish(self):
         r = self.rings()
-        for _, _, chain in self.sequences():
+        for chain in self.sequences():
             for name, step in chain:
-                self.ring_done(*r[name], step)
+                self.direct_done(*r[name]) if step == 0 else self.ring_done(*r[name], step)
+        self.direct_done(*r["z"])
         self.scatter_c_done()
         self.scatter_r_done()
         self.swap_done()
@@ -442,8 +457,8 @@
     dma = pltpu.SemaphoreType.DMA
     shapes = {
         "local": (6,), "cs_send": (SUB, nx * ny), "cs_recv": (SUB, 2), "rs_send": (nz,), "rs_recv": (),
-        "x0": (SUB, 2, 2, nx // 2), "y0": (SUB, 2, 2, ny // 2), "y1": (SUB, 2, 2, ny // 2), "x1": (SUB, 2, 2, nx // 2),
-        "z": (1, 2, 2, nz // 2), "swap": (2,), "d": (3,), "v_send": (4, nx + ny + 2 * nz - 4), "v_recv": (4, nz), "v_swap": (2, 4),
+        "x0": (2, nx), "y0": (2, 2, ny // 2), "y1": (2, ny), "x1": (2, 2, nx // 2),
+        "z": (2, nz), "swap": (2,), "d": (3,), "v_send": (4, nx + ny + 2 * nz - 3), "v_recv": (4, nz), "v_swap": (2, 4),
         "cv_recv": (ny,),
     }
     return [dma(shapes[name]) for name in NAMES]
@@ -601,10 +616,10 @@
     @pl.when(c.root)
     def _():
         def hook(j):
-            if j >= ROOT_LAG:
-                c.slot(j - ROOT_LAG)
+            for t in ROOT.get(j, ()):
+                c.slot(t)
         factor(c, s, begin, hook)
-        for t in range(8 - ROOT_LAG, slots):
+        for t in range(3, slots):
             c.slot(t)
 
     @pl.when(jnp.logical_not(c.root))
@@ -615,16 +630,18 @@
             for depth in (1, 2, 3):
                 for b in range(4):
                     if RELAY[depth][b] == t:
-                        pl.when(c.depth(depth))(lambda b=b: c.v_relay(b))
+                        pl.when(c.depth(depth, b))(lambda b=b: c.v_relay(b))
             for b in range(4):
                 if RELAY[4][b] == t:
                     c.v_collect(b)
-        for b in range(4):
-            c.v_wait(b)
-
-    for p in range(2):
-        panel_rows(c, p, pr, rcat)
-        panel_columns(c, p, ccat)
+    c.v_wait(0)
+    panel_rows(c, 0, pr, rcat)
+    panel_columns(c, 0, ccat)
+    pl.when(jnp.logical_not(c.root))(lambda: c.v_collect(3))
+    for b in range(1, 4):
+        c.v_wait(b)
+    panel_rows(c, 1, pr, rcat)
+    panel_columns(c, 1, ccat)
     update(c, out, pr, rcat, ccat)
     c.finish()
 

time: 78.2 us -> 75.5 us (0.965)
  the two profiles are of different devices: /device:TPU:37 before, /device:TPU:62 now
where the time goes in v3:
time: 75.5 us; the launch traced here: 75.3 us
  Pallas kernels  72.4 us (96%)
  local copies, waits for them, and re-layouts  2.91 us (4%)
    pallas_call x1, Pallas kernels, on_device(): pl.pallas_call(functools.partial(kernel, dims), out_shape=jax.ShapeDtypeS...  72.4 us
    unnamed x3, local copies, waits for them, and re-layouts  2.91 us

profile of v3, /device:TPU:62, one launch (start us, length us, event | category | flops | bytes accessed | tf_op | source)
XLA Modules:
  0.0 75.3 jit_solution(13634375843918723736)
XLA Ops:
  0.0 0.0 copy-start
  0.0 1.6 %copy-done = f32[2,256,4,256]{3,2,1,0:T(4,128)S(1)} copy-done((f32[2,256,4,256]{3,2,1,0:T(4,128)S(1)}, f32[2,256,4,256]{3,2,1,0:T(4,128)}, u32[]{:S(2)}) %copy-start) | copy-done | bytes 2097176
  1.6 72.4 %panels.1 = f32[4096,128]{1,0:T(8,128)S(1)} custom-call(f32[4096,128]{1,0:T(8,128)S(1)} %bitcast.11), custom_call_target="tpu_custom_call" | custom-call | tf_op jit(solution)/shard_map/panels/pallas_call | solution.py:654
  74.0 1.3 %copy.5 = f32[2,256,4,256]{3,2,1,0:T(4,128)} copy(f32[2,256,4,256]{3,2,1,0:T(4,128)S(1)} %bitcast.10) | data formatting | bytes 4194304
Async XLA Ops:
  0.0 1.6 %copy-start = (f32[2,256,4,256]{3,2,1,0:T(4,128)S(1)}, f32[2,256,4,256]{3,2,1,0:T(4,128)}, u32[]{:S(2)}) copy-start(f32[2,256,4,256]{3,2,1,0:T(4,128)} %param.1) | copy-start | bytes 6291460
